TPU v7x, 512 devices: a whole 4x8x8 slice. The times are simulated.
512 devices in a mesh: dp: 64 (over y, z), fsdp: 8 (over x, core).
Axes of the slice: x: 4, y: 8, z: 8, core: 2. Of those that a mesh axis runs over, the one named last changes fastest.
Arguments:
- teacher_feat: bfloat16 [16384, 256], P(('dp', 'fsdp')), may hold values from -1 to 1
- student_feat: bfloat16 [16384, 256], P(('dp', 'fsdp')), may hold values from -1 to 1
- crop_weight: bfloat16 [16384], P(('dp', 'fsdp')), may hold values from -96 to 96
- teacher_v: bfloat16 [256, 32768], P(None, 'fsdp'), may hold values from -2 to 2
- student_v: bfloat16 [256, 32768], P(None, 'fsdp'), may hold values from -2 to 2
Outputs:
- grad_v: float32 [256, 32768], P('dp', 'fsdp')
- grad_feat: float32 [16384, 256], P(('dp', 'fsdp'))
All inputs are finite; a program needn't handle non-finite values.
Results may differ from a plain program's by a relative error of at most 0.0073.
Values may be sent and summed in bfloat16 or wider, within the bound.
A program may use at most 64 MiB of HBM per device.

v0:
```python
import jax
import jax.numpy as jnp
from jax import lax
from jax.sharding import PartitionSpec as P

K = 32768
ITERS = 3


teacher_temp = 0.04
student_temp = 0.1
epsilon = 1e-06


def unit_rows(values):
    floats = values.astype(jnp.float32)
    length = jnp.sqrt(jnp.sum(floats * floats, axis=1, keepdims=True) + epsilon)
    return (floats / length, length)


def unit_columns(values):
    floats = values.astype(jnp.float32)
    length = jnp.sqrt(jnp.sum(floats * floats, axis=0, keepdims=True) + epsilon)
    return (floats / length, length)


def scale_prototypes(mass):
    proto_mass = lax.psum(jnp.sum(mass, axis=0), "dp")
    return mass / (proto_mass * K)[None, :]


def scale_crops(mass, crop_count):
    crop_mass = lax.psum(jnp.sum(mass, axis=1), "fsdp")
    return mass / (crop_mass * crop_count)[:, None]


def body(teacher_feat, student_feat, crop_weight, teacher_v, student_v):
    teacher_rows, student_rows, weight_rows = (
        lax.all_gather(teacher_feat, "fsdp", axis=0, tiled=True),
        lax.all_gather(student_feat, "fsdp", axis=0, tiled=True),
        lax.all_gather(crop_weight, "fsdp", axis=0, tiled=True),
    )
    local_rows = teacher_feat.shape[0]
    crop_count = teacher_rows.shape[0] * lax.axis_size("dp")
    teacher_hat, _ = unit_rows(teacher_rows)
    student_hat, student_len = unit_rows(student_rows)
    teacher_w, _ = unit_columns(teacher_v)
    student_w, student_wlen = unit_columns(student_v)
    student_unit = student_hat.astype(jnp.bfloat16)
    student_wunit = student_w.astype(jnp.bfloat16)
    teacher_mass = jnp.exp(
        jnp.dot(
            teacher_hat.astype(jnp.bfloat16),
            teacher_w.astype(jnp.bfloat16),
            preferred_element_type=jnp.float32,
        )
        / teacher_temp
    )
    student_mass = jnp.exp(
        jnp.dot(student_unit, student_wunit, preferred_element_type=jnp.float32) / student_temp
    )
    student_part = jnp.sum(student_mass, axis=1)
    student_total = lax.psum(student_part, "fsdp")
    first_sweep = 0
    for sweep_index in range(first_sweep, ITERS):
        teacher_mass = scale_prototypes(teacher_mass)
        teacher_mass = scale_crops(teacher_mass, crop_count)
    target = teacher_mass * crop_count
    student_prob = student_mass / student_total[:, None]
    gradient = (
        (student_prob - target) * weight_rows.astype(jnp.float32)[:, None] / student_temp
    ).astype(jnp.bfloat16)
    feature_part = lax.dot_general(
        gradient, student_wunit, (((1,), (1,)), ((), ())), preferred_element_type=jnp.float32
    )
    feature_grad = lax.psum(feature_part, "fsdp")
    first_row = lax.axis_index("fsdp") * local_rows
    own_grad = lax.dynamic_slice_in_dim(feature_grad, first_row, local_rows, 0)
    own_hat = lax.dynamic_slice_in_dim(student_hat, first_row, local_rows, 0)
    own_len = lax.dynamic_slice_in_dim(student_len, first_row, local_rows, 0)
    grad_feat = (own_grad - own_hat * jnp.sum(own_hat * own_grad, axis=1, keepdims=True)) / own_len
    weight_part = lax.dot_general(
        student_unit, gradient, (((0,), (0,)), ((), ())), preferred_element_type=jnp.float32
    )
    weight_grad = lax.psum_scatter(weight_part, "dp", scatter_dimension=0, tiled=True)
    slab_rows = weight_grad.shape[0]
    unit_slab = lax.dynamic_slice_in_dim(student_w, lax.axis_index("dp") * slab_rows, slab_rows, 0)
    weight_dot = lax.psum(jnp.sum(unit_slab * weight_grad, axis=0), "dp")
    grad_v = (weight_grad - unit_slab * weight_dot[None, :]) / student_wlen
    return (grad_v, grad_feat)


def solution(mesh):
    placed = (
        P(("dp", "fsdp"), None),
        P(("dp", "fsdp"), None),
        P(("dp", "fsdp")),
        P(None, "fsdp"),
        P(None, "fsdp"),
    )
    return jax.shard_map(
        body,
        mesh=mesh,
        in_specs=placed,
        out_specs=(P("dp", "fsdp"), P(("dp", "fsdp"), None)),
        check_vma=False,
    )
```

profile of v0, /device:TPU:6, one launch (start us, length us, event | category | flops | bytes accessed | tf_op | source)
XLA Modules:
  0.0 1473.7 jit_solution(11603462912581795662)
XLA Ops:
  7.2 15.7 %all_gather.10 = bf16[256,256]{1,0:T(8,128)(2,1)S(1)} all-gather(bf16[32,256]{1,0:T(8,128)(2,1)} %param.5), channel_id=1, replica_groups=mesh['dp'=64,'fsdp'=8] {'fsdp'}, dimensions={0}, use_global_device_ids=true | all-gather | bytes 147456 | tf_op jit(solution)/shard_map/all_gather | solution.py:39
  23.0 2.0 fusion.9
  25.1 4.7 fusion.31
  29.7 283.1 %psum.64 = f32[4096]{0:T(1024)S(1)} all-reduce(f32[4096]{0:T(1024)S(1)} %get-tuple-element.4), channel_id=1, replica_groups=mesh['dp'=64,'fsdp'=8] {'dp'}, use_global_device_ids=true, to_apply=%region_7.0 | all-reduce | flops 4096 | bytes 32768 | tf_op jit(solution)/shard_map/psum | solution.py:28
  312.9 2.6 divide_reduce_fusion
  315.4 10.0 psum.65
  325.5 3.0 fusion.14
  328.4 274.0 %psum.66 = f32[4096]{0:T(1024)S(1)} all-reduce(f32[4096]{0:T(1024)S(1)} %fusion.14), channel_id=1, replica_groups=mesh['dp'=64,'fsdp'=8] {'dp'}, use_global_device_ids=true, to_apply=%region_11.0 | all-reduce | flops 4096 | bytes 32768 | tf_op jit(solution)/shard_map/psum | solution.py:28
  602.4 3.0 fusion.15
  605.4 11.7 psum.67
  617.1 3.3 fusion.16
  620.5 274.0 %psum.68 = f32[4096]{0:T(1024)S(1)} all-reduce(f32[4096]{0:T(1024)S(1)} %fusion.16), channel_id=1, replica_groups=mesh['dp'=64,'fsdp'=8] {'dp'}, use_global_device_ids=true, to_apply=%region_15.0 | all-reduce | flops 4096 | bytes 32768 | tf_op jit(solution)/shard_map/psum | solution.py:28
  894.4 3.4 fusion.17
  897.8 13.5 all_gather.9
  911.9 3.1 fusion.32
  915.0 11.9 all-reduce.2
  929.1 12.7 all-reduce
  941.7 4.5 multiply_convert_fusion
  947.6 1.7 fusion.20
  949.4 4.3 fusion.28
  955.8 2.5 convert_divide_fusion.1
  958.4 53.7 %all-reduce.6.cloned.1.call-done = f32[256,256]{1,0:T(8,128)} async-done(((f32[256,256]{1,0:T(8,128)}), f32[256,256]{1,0:T(8,128)}) %all-reduce.6.cloned.1.call-update) | async-done | bytes 262160 | tf_op jit(solution)/shard_map/psum | solution.py:76
  1014.4 172.8 %all-reduce.8.cloned.1.call-done = f32[256,4096]{1,0:T(8,128)} async-done(((f32[256,4096]{1,0:T(8,128)}), f32[256,4096]{1,0:T(8,128)}) %all-reduce.8.cloned.1.call-update) | async-done | bytes 4194320
  1188.2 277.1 %psum.70 = f32[4096]{0:T(1024)S(1)} all-reduce(f32[4096]{0:T(1024)S(1)} %multiply_reduce_fusion), channel_id=1, replica_groups=mesh['dp'=64,'fsdp'=8] {'dp'}, use_global_device_ids=true, to_apply=%region_20.0 | all-reduce | flops 4096 | bytes 32768 | tf_op jit(solution)/shard_map/psum | solution.py:88
  (36 shorter events, 10.1 us)
Async XLA Ops:
  7.2 1004.9 %all-reduce.6.cloned.1.call-start = ((), (), s32[]{:S(2)}) async-start(), calls=%async_computation | async-start | bytes 524288 | tf_op jit(solution)/shard_map/psum | solution.py:76
  617.1 280.6 %copy-start.2 = (bf16[32,256]{1,0:T(8,128)(2,1)S(1)}, bf16[32,256]{1,0:T(8,128)(2,1)}, u32[]{:S(2)}) copy-start(bf16[32,256]{1,0:T(8,128)(2,1)} %param.6) | copy-start | bytes 49156
  617.1 294.3 %copy-start = (bf16[256,4096]{1,0:T(8,128)(2,1)S(1)}, bf16[256,4096]{1,0:T(8,128)(2,1)}, u32[]{:S(2)}) copy-start(bf16[256,4096]{1,0:T(8,128)(2,1)} %param.9) | copy-start | bytes 6291460
  911.9 16.9 %copy-start.3 = (bf16[32]{0:T(256)(128)(2,1)S(1)}, bf16[32]{0:T(256)(128)(2,1)}, u32[]{:S(2)}) copy-start(bf16[32]{0:T(256)(128)(2,1)} %param.7) | copy-start | bytes 196
  946.3 1.3 copy-start.1
  949.3 237.8 %all-reduce.8.cloned.1.call-start = ((), (), s32[]{:S(2)}) async-start(), calls=%async_computation.1 | async-start | bytes 8388608
Sparse Core Ops, SparseCore 0:
  949.4 62.5 all-reduce.5
  1015.7 171.4 all-reduce.7
where the time goes:
time: 1470 us
  blocking collectives  1180 us (80%)
  waiting for transfers between devices  226 us (15%)
  other arithmetic  30.1 us (2%)
  between operations  15.5 us (1%)
    psum x3, blocking collectives, scale_prototypes(): proto_mass = lax.psum(jnp.sum(mass, axis=0), 'dp')  831 us
    psum x1, blocking collectives, body(): weight_dot = lax.psum(jnp.sum(unit_slab * weight_grad, axis=0), 'dp')  277 us
    unnamed x3, waiting for transfers between devices  173 us
    psum x1, waiting for transfers between devices, body(): feature_grad = lax.psum(feature_part, 'fsdp')  53.7 us
    psum x3, blocking collectives, scale_crops(): crop_mass = lax.psum(jnp.sum(mass, axis=1), 'fsdp')  33.6 us
  transfers between devices with their start and end apart: 2, of which 2 were waited for; matrix products, arithmetic and copies ran while one was open for 1% of the time, Pallas kernels for 0%

commit v1 on v0

v1 whole, which is shorter than its diff:
```python
import functools

import jax
import jax.numpy as jnp
from jax import lax
from jax.experimental import pallas as pl
from jax.experimental.pallas import tpu as pltpu
from jax.sharding import PartitionSpec as P

K = 32768
ITERS = 3
BLOCKS = 16
HALF = BLOCKS // 2

teacher_temp = 0.04
student_temp = 0.1
epsilon = 1e-06
F32 = jnp.float32
BF16 = jnp.bfloat16
MESH = pl.DeviceIdType.MESH


def far_first(n):
    return sorted(range(1, n), key=lambda j: -min(j, n - j))


def lanes_of(partial):
    return jnp.sum(jnp.transpose(partial), axis=0, keepdims=True)


def rows_of(vector, width):
    return jnp.transpose(jnp.broadcast_to(vector, (width, vector.shape[1])))


def dot_nt(a, b):
    return lax.dot_general(a, b, (((1,), (1,)), ((), ())), preferred_element_type=F32)


def dot_nn(a, b):
    return jnp.dot(a, b, preferred_element_type=F32)


def kernel(
    geo,
    tf_hbm, sf_hbm, cw_ref, tv_hbm, sv_hbm,
    gv_ref, gf_ref,
    tf, sf, tv, sv, sw, tu, su, sut, perm, mass, prob, winv, svec, rb, ab, bb, fg,
    col_own, col_recv, row_own, row_recv, st_own, st_recv,
    part, ring_recv, second, second_recv, fg_recv,
    local_sem, gather_send, gather_recv, col_send, col_got, row_send, row_got, st_send, st_got,
    ring_send, ring_got, second_send, second_got, fg_send, fg_got,
):
    ny, nz, nf = geo
    local = tf.shape[0]
    bot = tv.shape[0]
    kl = tv.shape[1]
    rows = local * nf
    cb = kl // BLOCKS
    crops = rows * ny * nz
    protos = kl * nf
    dp, f = lax.axis_index("dp"), lax.axis_index("fsdp")
    y, z = dp // nz, lax.rem(dp, nz)

    def on_y(j):
        return {"dp": lax.rem(y + j, ny) * nz + z}

    def on_z(j):
        return {"dp": y * nz + lax.rem(z + j, nz)}

    def on_f(j):
        return {"fsdp": lax.rem(f + j, nf)}

    axes = ((on_y, ny, y), (on_z, nz, z))

    def block(j):
        return pl.ds(pl.multiple_of(j * cb, cb), cb)

    def send(src, dst, send_sem, recv_sem, device):
        pltpu.make_async_remote_copy(
            src_ref=src, dst_ref=dst, send_sem=send_sem, recv_sem=recv_sem,
            device_id=device, device_id_type=MESH,
        ).start()

    def took(ref, sem):
        pltpu.make_async_copy(ref, ref, sem).wait()

    loads = [
        pltpu.make_async_copy(src, dst, local_sem.at[i])
        for i, (src, dst) in enumerate(((tf_hbm, tf), (sf_hbm, sf), (tv_hbm, tv), (sv_hbm, sv)))
    ]
    for load in loads:
        load.start()
    barrier = pltpu.get_barrier_semaphore()
    for axis, n in ((on_f, nf), (on_y, ny), (on_z, nz)):
        for j in far_first(n):
            pl.semaphore_signal(barrier, inc=1, device_id=axis(j), device_id_type=MESH)

    own = pl.ds(pl.multiple_of(f * local, local), local)

    def unit_rows(ref):
        values = ref[...].astype(F32)
        length = jnp.sqrt(jnp.sum(values * values, axis=1, keepdims=True) + epsilon)
        return values / length, length

    loads[0].wait()
    tu[own, :] = unit_rows(tf)[0].astype(BF16)
    loads[1].wait()
    su[own, :] = unit_rows(sf)[0].astype(BF16)
    pl.semaphore_wait(barrier, nf + ny + nz - 3)
    for i, unit in enumerate((tu, su)):
        for j in far_first(nf):
            send(unit.at[own], unit.at[own], gather_send.at[i], gather_recv.at[i], on_f(j))
    others = pl.ds(0, rows - local)

    loads[2].wait()

    @pl.loop(0, BLOCKS)
    def _(j):
        values = tv[:, block(j)].astype(F32)
        inverse = 1.0 / jnp.sqrt(jnp.sum(values * values, axis=0, keepdims=True) + epsilon)
        tv[:, block(j)] = (values * inverse).astype(BF16)

    def student_prototypes():
        loads[3].wait()

        @pl.loop(0, BLOCKS)
        def _(j):
            values = sv[:, block(j)].astype(F32)
            inverse = 1.0 / jnp.sqrt(jnp.sum(values * values, axis=0, keepdims=True) + epsilon)
            winv[pl.ds(j, 1), :] = inverse
            sw[:, block(j)] = (values * inverse).astype(BF16)

    def student_orders():
        each = bot // (ny * nz)
        p = lax.broadcasted_iota(jnp.int32, (bot, bot), 0)
        d = lax.broadcasted_iota(jnp.int32, (bot, bot), 1)
        pz, py, pi = p // (ny * each), lax.rem(p // each, ny), lax.rem(p, each)
        perm[...] = (d == (py * nz + pz) * each + pi).astype(F32).astype(BF16)
        took(su.at[others], gather_recv.at[1])
        units = su[...]
        sut[0] = dot_nt((d == p).astype(F32).astype(BF16), units).astype(BF16)
        sut[1] = dot_nt(perm[...], units).astype(BF16)

        @pl.loop(HALF, BLOCKS)
        def _(j):
            sv[:, block(j)] = dot_nn(perm[...], sv[:, block(j)]).astype(BF16)

    def student_mass():
        def step(j, total):
            values = jnp.exp(dot_nn(su[...], sw[:, block(j)]) * (1.0 / student_temp))
            prob[j] = values
            for c in range(0, cb, 128):
                total = total + values[:, c : c + 128]
            return total

        total = lax.fori_loop(0, BLOCKS, step, jnp.zeros((rows, 128), F32))
        st_own[0] = lanes_of(total)
        i = lax.broadcasted_iota(jnp.int32, (local, rows), 0)
        c = lax.broadcasted_iota(jnp.int32, (local, rows), 1)
        place = (c == f * local + i).astype(F32).astype(BF16)
        st_own[1] = dot_nn(cw_ref[...], place)
        for j in far_first(nf):
            send(st_own, st_recv.at[j - 1], st_send, st_got, on_f(j))

    def col_first(it, h):
        axis, n, _ = axes[h]
        for j in far_first(n):
            send(col_own.at[it, h, 0], col_recv.at[it, h, 0, j - 1], col_send.at[it, h, 0], col_got.at[it, h, 0], axis(j))

    def col_total(it, h, stage):
        n = axes[(h + stage) % 2][1]
        took(col_recv.at[it, h, stage], col_got.at[it, h, stage])
        total = col_own[it, h, stage]
        for j in range(n - 1):
            total = total + col_recv[it, h, stage, j]
        return total

    def col_second(it, h):
        col_own[it, h, 1] = col_total(it, h, 0)
        axis, n, _ = axes[1 - h]
        for j in far_first(n):
            send(col_own.at[it, h, 1], col_recv.at[it, h, 1, j - 1], col_send.at[it, h, 1], col_got.at[it, h, 1], axis(j))

    took(tu.at[others], gather_recv.at[0])
    for it in range(ITERS):
        for h in range(2):

            @pl.loop(0, HALF)
            def _(k):
                j = h * HALF + k
                if it == 0:
                    values = jnp.exp(dot_nn(tu[...], tv[:, block(j)]) * (1.0 / teacher_temp))
                    mass[j] = values
                else:
                    values = mass[j] * rb[...]
                col_own[it, h, 0, pl.ds(k, 1), :] = jnp.sum(values, axis=0, keepdims=True)

            col_first(it, h)
        if it == 0:
            student_prototypes()
        if it == 1:
            student_mass()
        for h in range(2):
            col_second(it, h)
        if it == 0:
            student_orders()
        total = jnp.zeros((rows, 128), F32)
        for h in range(2):
            svec[h * HALF : (h + 1) * HALF, :] = 1.0 / (col_total(it, h, 1) * protos)

            def row_step(k, total):
                j = h * HALF + k
                values = mass[j] * svec[pl.ds(j, 1), :]
                for c in range(0, cb, 128):
                    total = total + values[:, c : c + 128]
                return total

            total = lax.fori_loop(0, HALF, row_step, total)
        row_own[it] = lanes_of(total)
        for j in far_first(nf):
            send(row_own.at[it], row_recv.at[it, j - 1], row_send.at[it], row_got.at[it], on_f(j))
        if it == ITERS - 1:
            took(st_recv, st_got)
            student_total, weights = st_own[0], st_own[1]
            for j in range(nf - 1):
                student_total = student_total + st_recv[j, 0]
                weights = weights + st_recv[j, 1]
            ab[...] = rows_of(weights / (student_total * student_temp), cb)
        took(row_recv.at[it], row_got.at[it])
        row_total = row_own[it]
        for j in range(nf - 1):
            row_total = row_total + row_recv[it, j]
        if it < ITERS - 1:
            rb[...] = rows_of(1.0 / (row_total * crops), cb)
        else:
            bb[...] = rows_of(weights / (row_total * student_temp), cb)

    fg[...] = jnp.zeros_like(fg)
    rings = [(h, way, sub) for sub in range(2) for way in range(2) for h in range(2)]

    def ring_id(h, way, sub):
        return h * 4 + way * 2 + sub

    def chunk(h, c):
        size = bot // axes[h][1]
        return pl.ds(pl.multiple_of(c * size, size), size)

    def ring_step(h, way, sub, s):
        axis, n, me = axes[h]
        r = ring_id(h, way, sub)
        ahead = 1 if way == 0 else n - 1
        c = lax.rem(me + (n - 1 - s if way == 0 else 1 + s), n)
        if s > 0:
            took(ring_recv.at[r, s - 1], ring_got.at[r, s - 1])
            part[r, chunk(h, c), :] = part[r, chunk(h, c), :] + ring_recv[r, s - 1]
        send(part.at[r, chunk(h, c)], ring_recv.at[r, s], ring_send.at[r], ring_got.at[r, s], axis(ahead))

    for h, way, sub in rings:
        r = ring_id(h, way, sub)
        for k in range(2):
            j = 2 * r + k
            g = (prob[j] * ab[...] - mass[j] * bb[...] * svec[j : j + 1, :]).astype(BF16)
            columns = slice(j * cb, (j + 1) * cb)
            fg[...] += dot_nt(g, sw[:, columns])
            grad = dot_nn(sut[h], g)
            inverse = winv[j : j + 1, :]
            w = sv[:, columns].astype(F32) * inverse
            inner = jnp.sum(w * grad, axis=0, keepdims=True)
            part[r, :, k * cb : (k + 1) * cb] = ((grad - w * inner) * inverse).astype(BF16)
        ring_step(h, way, sub, 0)

    def rows_at(i):
        return pl.ds(pl.multiple_of(i * local, local), local)

    for j in far_first(nf):
        send(fg.at[rows_at(lax.rem(f + j, nf))], fg_recv.at[j - 1], fg_send, fg_got, on_f(j))
    for s in range(1, max(ny, nz) - 1):
        for h, way, sub in rings:
            if s < axes[h][1] - 1:
                ring_step(h, way, sub, s)

    each = bot // (ny * nz)
    for h in range(2):
        _, n, me = axes[h]
        sums = []
        for way in range(2):
            for sub in range(2):
                r = ring_id(h, way, sub)
                took(ring_recv.at[r, n - 2], ring_got.at[r, n - 2])
                sums.append(part[r, chunk(h, me), :].astype(F32) + ring_recv[r, n - 2].astype(F32))
        axis, n2, me2 = axes[1 - h]
        for c in range(n2):
            second[h, c] = jnp.concatenate([total[c * each : (c + 1) * each] for total in sums], axis=0).astype(BF16)
        for j in far_first(n2):
            send(second.at[h, lax.rem(me2 + j, n2)], second_recv.at[h, j - 1], second_send.at[h], second_got.at[h], axis(j))

    took(fg_recv, fg_got)
    grad = fg[rows_at(f), :]
    for j in range(nf - 1):
        grad = grad + fg_recv[j]
    hat, length = unit_rows(sf)
    gf_ref[...] = (grad - hat * jnp.sum(hat * grad, axis=1, keepdims=True)) / length

    for h in range(2):
        took(second_recv.at[h], second_got.at[h])
        _, n2, me2 = axes[1 - h]
        total = second[h, me2].astype(F32)
        for j in range(n2 - 1):
            total = total + second_recv[h, j].astype(F32)
        for q in range(4):
            first = h * HALF * cb + q * 2 * cb
            gv_ref[:, first : first + 2 * cb] = total[q * each : (q + 1) * each]

    for i, unit in enumerate((tu, su)):
        took(unit.at[others], gather_send.at[i])
    for it in range(ITERS):
        for h in range(2):
            for stage in range(2):
                took(col_recv.at[it, h, stage], col_send.at[it, h, stage])
        took(row_recv.at[it], row_send.at[it])
    took(st_recv, st_send)
    took(fg_recv, fg_send)
    for h in range(2):
        for way in range(2):
            for sub in range(2):
                r = ring_id(h, way, sub)
                took(ring_recv.at[r], ring_send.at[r])
        took(second_recv.at[h], second_send.at[h])


def step(geo, teacher_feat, student_feat, crop_weight, teacher_v, student_v):
    ny, nz, nf = geo
    local, bot = teacher_feat.shape
    kl = teacher_v.shape[1]
    rows, cb = local * nf, kl // BLOCKS
    each = bot // (ny * nz)
    any_space = pl.BlockSpec(memory_space=pl.ANY)
    vmem = pl.BlockSpec(memory_space=pltpu.VMEM)
    dma = pltpu.SemaphoreType.DMA
    return pl.pallas_call(
        functools.partial(kernel, geo),
        out_shape=(
            jax.ShapeDtypeStruct((each, kl), F32),
            jax.ShapeDtypeStruct((local, bot), F32),
        ),
        in_specs=[any_space, any_space, vmem, any_space, any_space],
        out_specs=(vmem, vmem),
        scratch_shapes=[
            pltpu.VMEM((local, bot), BF16),
            pltpu.VMEM((local, bot), BF16),
            pltpu.VMEM((bot, kl), BF16),
            pltpu.VMEM((bot, kl), BF16),
            pltpu.VMEM((bot, kl), BF16),
            pltpu.VMEM((rows, bot), BF16),
            pltpu.VMEM((rows, bot), BF16),
            pltpu.VMEM((2, bot, rows), BF16),
            pltpu.VMEM((bot, bot), BF16),
            pltpu.VMEM((BLOCKS, rows, cb), F32),
            pltpu.VMEM((BLOCKS, rows, cb), F32),
            pltpu.VMEM((BLOCKS, cb), F32),
            pltpu.VMEM((BLOCKS, cb), F32),
            pltpu.VMEM((rows, cb), F32),
            pltpu.VMEM((rows, cb), F32),
            pltpu.VMEM((rows, cb), F32),
            pltpu.VMEM((rows, bot), F32),
            pltpu.VMEM((ITERS, 2, 2, HALF, cb), F32),
            pltpu.VMEM((ITERS, 2, 2, ny - 1, HALF, cb), F32),
            pltpu.VMEM((ITERS, 1, rows), F32),
            pltpu.VMEM((ITERS, nf - 1, 1, rows), F32),
            pltpu.VMEM((2, 1, rows), F32),
            pltpu.VMEM((nf - 1, 2, 1, rows), F32),
            pltpu.VMEM((8, bot, 2 * cb), BF16),
            pltpu.VMEM((8, ny - 1, bot // ny, 2 * cb), BF16),
            pltpu.VMEM((2, ny, 4 * each, 2 * cb), BF16),
            pltpu.VMEM((2, ny - 1, 4 * each, 2 * cb), BF16),
            pltpu.VMEM((nf - 1, local, bot), F32),
            dma((4,)),
            dma((2,)), dma((2,)),
            dma((ITERS, 2, 2)), dma((ITERS, 2, 2)),
            dma((ITERS,)), dma((ITERS,)),
            dma, dma,
            dma((8,)), dma((8, ny - 1)),
            dma((2,)), dma((2,)),
            dma, dma,
        ],
        compiler_params=pltpu.CompilerParams(
            collective_id=0, has_side_effects=True, vmem_limit_bytes=48 * 1024 * 1024
        ),
    )(teacher_feat, student_feat, crop_weight.reshape(1, local), teacher_v, student_v)


def solution(mesh, planes=(8, 8)):
    geo = (*planes, mesh.shape["fsdp"])
    placed = (
        P(("dp", "fsdp"), None),
        P(("dp", "fsdp"), None),
        P(("dp", "fsdp")),
        P(None, "fsdp"),
        P(None, "fsdp"),
    )
    return jax.shard_map(
        functools.partial(step, geo),
        mesh=mesh,
        in_specs=placed,
        out_specs=(P("dp", "fsdp"), P(("dp", "fsdp"), None)),
        check_vma=False,
    )
```

time: 1470 us -> 103 us (0.07)
  blocking collectives: 1180 us -> 0 us
  waiting for transfers between devices: 226 us -> 0 us
  Pallas kernels: 0 us -> 94.7 us
  other arithmetic: 30.1 us -> 0 us
  between operations: 15.5 us -> 0.65 us
    psum x7 -> x0, blocking collectives: 1140 us -> none  [the longest x3 831 us: scale_prototypes(): proto_mass = lax.psum(jnp.sum(mass, axis=0), 'dp')]
    unnamed x3 -> x0, waiting for transfers between devices: 173 us -> none
    pallas_call x0 -> x1, Pallas kernels: none -> 94.7 us  [step(): pl.pallas_call(functools.partial(kernel, geo), out_shape=(jax.ShapeDtypeS...]
    psum x1 -> x0, waiting for transfers between devices: 53.7 us -> none  [body(): feature_grad = lax.psum(feature_part, 'fsdp')]
    all_gather x2 -> x0, blocking collectives: 29.2 us -> none  [the longest x1 15.7 us: body(): lax.all_gather(teacher_feat, 'fsdp', axis=0, tiled=True)]
    reduce_sum x11 -> x0, other arithmetic: 19.8 us -> none  [the longest x3 8.94 us: scale_crops(): crop_mass = lax.psum(jnp.sum(mass, axis=1), 'fsdp')]
  transfers between devices with their start and end apart: 2 -> 0, of which waited for: 2 -> 0; matrix products, arithmetic and copies ran while one was open for 1% -> 0% of each run, Pallas kernels for 0% -> 0%
where the time goes in v1:
time: 103 us; the launch traced here: 102 us
  Pallas kernels  94.7 us (92%)
  local copies, waits for them, and re-layouts  6.51 us (6%)
    pallas_call x1, Pallas kernels, step(): pl.pallas_call(functools.partial(kernel, geo), out_shape=(jax.ShapeDtypeS...  94.7 us
    unnamed x12, local copies, waits for them, and re-layouts  6.51 us

profile of v1, /device:TPU:6, one launch (start us, length us, event | category | flops | bytes accessed | tf_op | source)
XLA Modules:
  0.0 101.8 jit_solution(3004684133678379923)
XLA Ops:
  0.6 0.0 copy-start
  0.6 1.6 %copy-done = bf16[256,4096]{1,0:T(8,128)(2,1)S(1)} copy-done((bf16[256,4096]{1,0:T(8,128)(2,1)S(1)}, bf16[256,4096]{1,0:T(8,128)(2,1)}, u32[]{:S(2)}) %copy-start) | copy-done | bytes 2097176
  2.2 0.0 copy-start.1
  2.2 1.6 %copy-done.1 = bf16[256,4096]{1,0:T(8,128)(2,1)S(1)} copy-done((bf16[256,4096]{1,0:T(8,128)(2,1)S(1)}, bf16[256,4096]{1,0:T(8,128)(2,1)}, u32[]{:S(2)}) %copy-start.1) | copy-done | bytes 2097176
  3.8 0.0 copy-start.2
  3.8 0.7 copy-done.2
  4.5 0.0 copy-start.3
  4.5 0.7 copy-done.3
  5.3 0.0 copy-start.4
  5.3 0.7 copy-done.4
  5.9 94.7 %shard_map.68 = (f32[4,4096]{1,0:T(4,128)S(1)}, f32[32,256]{1,0:T(8,128)S(1)}) custom-call(bf16[32,256]{1,0:T(8,128)(2,1)S(1)} %copy-done.2, bf16[32,256]{1,0:T(8,128)(2,1)S(1)} %copy-done.3, bf16[1,32]{1,0:T(2,128)(2,1)S(1)} %bitcast.1, bf16[256,4096]{1,0:T(8,128)(2,1)S(1)} %copy-done, bf16[256,4096]{1,0:T(8,128)(2,1)S(1)} %copy-done.1), custom_call_target="tpu_custom_call" | custom-call | tf_op jit(solution)/shard_map/pallas_call | solution.py:340
  100.6 0.6 copy.9
  101.2 0.6 copy.10
Async XLA Ops:
  0.6 1.6 %copy-start = (bf16[256,4096]{1,0:T(8,128)(2,1)S(1)}, bf16[256,4096]{1,0:T(8,128)(2,1)}, u32[]{:S(2)}) copy-start(bf16[256,4096]{1,0:T(8,128)(2,1)} %tv_hbm.1) | copy-start | bytes 6291460
  2.2 1.6 %copy-start.1 = (bf16[256,4096]{1,0:T(8,128)(2,1)S(1)}, bf16[256,4096]{1,0:T(8,128)(2,1)}, u32[]{:S(2)}) copy-start(bf16[256,4096]{1,0:T(8,128)(2,1)} %sv_hbm.1) | copy-start | bytes 6291460
  3.8 0.7 copy-start.2
  4.5 0.7 copy-start.3
  5.3 0.7 copy-start.4

commit v2 on v1

--- a/solution.py
+++ b/solution.py
@@ -73,7 +73,7 @@
     axes = ((on_y, ny, y), (on_z, nz, z))
 
     def block(j):
-        return pl.ds(pl.multiple_of(j * cb, cb), cb)
+        return slice(j * cb, (j + 1) * cb)
 
     def send(src, dst, send_sem, recv_sem, device):
         pltpu.make_async_remote_copy(
@@ -107,27 +107,26 @@
     loads[1].wait()
     su[own, :] = unit_rows(sf)[0].astype(BF16)
     pl.semaphore_wait(barrier, nf + ny + nz - 3)
-    for i, unit in enumerate((tu, su)):
+
+    def gather(i, unit):
         for j in far_first(nf):
             send(unit.at[own], unit.at[own], gather_send.at[i], gather_recv.at[i], on_f(j))
+
+    gather(0, tu)
     others = pl.ds(0, rows - local)
 
     loads[2].wait()
-
-    @pl.loop(0, BLOCKS)
-    def _(j):
+    for j in range(BLOCKS):
         values = tv[:, block(j)].astype(F32)
         inverse = 1.0 / jnp.sqrt(jnp.sum(values * values, axis=0, keepdims=True) + epsilon)
         tv[:, block(j)] = (values * inverse).astype(BF16)
 
     def student_prototypes():
         loads[3].wait()
-
-        @pl.loop(0, BLOCKS)
-        def _(j):
+        for j in range(BLOCKS):
             values = sv[:, block(j)].astype(F32)
             inverse = 1.0 / jnp.sqrt(jnp.sum(values * values, axis=0, keepdims=True) + epsilon)
-            winv[pl.ds(j, 1), :] = inverse
+            winv[j : j + 1, :] = inverse
             sw[:, block(j)] = (values * inverse).astype(BF16)
 
     def student_orders():
@@ -140,20 +139,16 @@
         units = su[...]
         sut[0] = dot_nt((d == p).astype(F32).astype(BF16), units).astype(BF16)
         sut[1] = dot_nt(perm[...], units).astype(BF16)
-
-        @pl.loop(HALF, BLOCKS)
-        def _(j):
+        for j in range(HALF, BLOCKS):
             sv[:, block(j)] = dot_nn(perm[...], sv[:, block(j)]).astype(BF16)
 
     def student_mass():
-        def step(j, total):
+        total = jnp.zeros((rows, 128), F32)
+        for j in range(BLOCKS):
             values = jnp.exp(dot_nn(su[...], sw[:, block(j)]) * (1.0 / student_temp))
             prob[j] = values
             for c in range(0, cb, 128):
                 total = total + values[:, c : c + 128]
-            return total
-
-        total = lax.fori_loop(0, BLOCKS, step, jnp.zeros((rows, 128), F32))
         st_own[0] = lanes_of(total)
         i = lax.broadcasted_iota(jnp.int32, (local, rows), 0)
         c = lax.broadcasted_iota(jnp.int32, (local, rows), 1)
@@ -181,41 +176,34 @@
         for j in far_first(n):
             send(col_own.at[it, h, 1], col_recv.at[it, h, 1, j - 1], col_send.at[it, h, 1], col_got.at[it, h, 1], axis(j))
 
+    student_prototypes()
     took(tu.at[others], gather_recv.at[0])
+    gather(1, su)
     for it in range(ITERS):
         for h in range(2):
-
-            @pl.loop(0, HALF)
-            def _(k):
+            for k in range(HALF):
                 j = h * HALF + k
                 if it == 0:
                     values = jnp.exp(dot_nn(tu[...], tv[:, block(j)]) * (1.0 / teacher_temp))
                     mass[j] = values
                 else:
                     values = mass[j] * rb[...]
-                col_own[it, h, 0, pl.ds(k, 1), :] = jnp.sum(values, axis=0, keepdims=True)
+                col_own[it, h, 0, k : k + 1, :] = jnp.sum(values, axis=0, keepdims=True)
 
             col_first(it, h)
         if it == 0:
-            student_prototypes()
-        if it == 1:
-            student_mass()
+            student_orders()
         for h in range(2):
             col_second(it, h)
         if it == 0:
-            student_orders()
+            student_mass()
         total = jnp.zeros((rows, 128), F32)
         for h in range(2):
             svec[h * HALF : (h + 1) * HALF, :] = 1.0 / (col_total(it, h, 1) * protos)
-
-            def row_step(k, total):
-                j = h * HALF + k
-                values = mass[j] * svec[pl.ds(j, 1), :]
+            for j in range(h * HALF, (h + 1) * HALF):
+                values = mass[j] * svec[j : j + 1, :]
                 for c in range(0, cb, 128):
                     total = total + values[:, c : c + 128]
-                return total
-
-            total = lax.fori_loop(0, HALF, row_step, total)
         row_own[it] = lanes_of(total)
         for j in far_first(nf):
             send(row_own.at[it], row_recv.at[it, j - 1], row_send.at[it], row_got.at[it], on_f(j))
@@ -236,58 +224,71 @@
             bb[...] = rows_of(weights / (row_total * student_temp), cb)
 
     fg[...] = jnp.zeros_like(fg)
-    rings = [(h, way, sub) for sub in range(2) for way in range(2) for h in range(2)]
-
-    def ring_id(h, way, sub):
-        return h * 4 + way * 2 + sub
+    rings = [(h, q) for q in range(4) for h in range(2)]
 
     def chunk(h, c):
         size = bot // axes[h][1]
         return pl.ds(pl.multiple_of(c * size, size), size)
 
-    def ring_step(h, way, sub, s):
+    def lengths(h, q):
+        n = axes[h][1]
+        return (n // 2, (n - 1) // 2) if q % 2 == 0 else ((n - 1) // 2, n // 2)
+
+    def chain_slot(h, q, way, s):
+        return s if way == 0 else lengths(h, q)[0] + s
+
+    def chain_step(h, q, way, s):
         axis, n, me = axes[h]
-        r = ring_id(h, way, sub)
-        ahead = 1 if way == 0 else n - 1
-        c = lax.rem(me + (n - 1 - s if way == 0 else 1 + s), n)
+        r = 4 * h + q
+        left = lengths(h, q)[way] - s
+        c = lax.rem(me + (left if way == 0 else n - left), n)
         if s > 0:
-            took(ring_recv.at[r, s - 1], ring_got.at[r, s - 1])
-            part[r, chunk(h, c), :] = part[r, chunk(h, c), :] + ring_recv[r, s - 1]
-        send(part.at[r, chunk(h, c)], ring_recv.at[r, s], ring_send.at[r], ring_got.at[r, s], axis(ahead))
-
-    for h, way, sub in rings:
-        r = ring_id(h, way, sub)
+            before = chain_slot(h, q, way, s - 1)
+            took(ring_recv.at[r, before], ring_got.at[r, before])
+            part[r, chunk(h, c), :] = part[r, chunk(h, c), :] + ring_recv[r, before]
+        now = chain_slot(h, q, way, s)
+        send(part.at[r, chunk(h, c)], ring_recv.at[r, now], ring_send.at[r], ring_got.at[r, now], axis(1 if way == 0 else n - 1))
+
+    def chain_steps(h, q, s):
+        for way in (0, 1) if q % 2 == 0 else (1, 0):
+            if s < lengths(h, q)[way]:
+                chain_step(h, q, way, s)
+
+    for h, q in rings:
+        r = 4 * h + q
         for k in range(2):
             j = 2 * r + k
             g = (prob[j] * ab[...] - mass[j] * bb[...] * svec[j : j + 1, :]).astype(BF16)
-            columns = slice(j * cb, (j + 1) * cb)
-            fg[...] += dot_nt(g, sw[:, columns])
+            fg[...] += dot_nt(g, sw[:, block(j)])
             grad = dot_nn(sut[h], g)
             inverse = winv[j : j + 1, :]
-            w = sv[:, columns].astype(F32) * inverse
+            w = sv[:, block(j)].astype(F32) * inverse
             inner = jnp.sum(w * grad, axis=0, keepdims=True)
             part[r, :, k * cb : (k + 1) * cb] = ((grad - w * inner) * inverse).astype(BF16)
-        ring_step(h, way, sub, 0)
+        chain_steps(h, q, 0)
 
     def rows_at(i):
         return pl.ds(pl.multiple_of(i * local, local), local)
 
     for j in far_first(nf):
         send(fg.at[rows_at(lax.rem(f + j, nf))], fg_recv.at[j - 1], fg_send, fg_got, on_f(j))
-    for s in range(1, max(ny, nz) - 1):
-        for h, way, sub in rings:
-            if s < axes[h][1] - 1:
-                ring_step(h, way, sub, s)
+    for s in range(1, max(ny, nz) // 2):
+        for h, q in rings:
+            chain_steps(h, q, s)
 
     each = bot // (ny * nz)
     for h in range(2):
         _, n, me = axes[h]
         sums = []
-        for way in range(2):
-            for sub in range(2):
-                r = ring_id(h, way, sub)
-                took(ring_recv.at[r, n - 2], ring_got.at[r, n - 2])
-                sums.append(part[r, chunk(h, me), :].astype(F32) + ring_recv[r, n - 2].astype(F32))
+        for q in range(4):
+            r = 4 * h + q
+            total = part[r, chunk(h, me), :].astype(F32)
+            for way in range(2):
+                if lengths(h, q)[way]:
+                    last = chain_slot(h, q, way, lengths(h, q)[way] - 1)
+                    took(ring_recv.at[r, last], ring_got.at[r, last])
+                    total = total + ring_recv[r, last].astype(F32)
+            sums.append(total)
         axis, n2, me2 = axes[1 - h]
         for c in range(n2):
             second[h, c] = jnp.concatenate([total[c * each : (c + 1) * each] for total in sums], axis=0).astype(BF16)
@@ -321,10 +322,8 @@
     took(st_recv, st_send)
     took(fg_recv, fg_send)
     for h in range(2):
-        for way in range(2):
-            for sub in range(2):
-                r = ring_id(h, way, sub)
-                took(ring_recv.at[r], ring_send.at[r])
+        for r in range(4 * h, 4 * h + 4):
+            took(ring_recv.at[r], ring_send.at[r])
         took(second_recv.at[h], second_send.at[h])
 
 
@@ -384,7 +383,7 @@
             dma, dma,
         ],
         compiler_params=pltpu.CompilerParams(
-            collective_id=0, has_side_effects=True, vmem_limit_bytes=48 * 1024 * 1024
+            collective_id=0, has_side_effects=True, vmem_limit_bytes=62 * 1024 * 1024
         ),
     )(teacher_feat, student_feat, crop_weight.reshape(1, local), teacher_v, student_v)
 

time: 103 us -> 86.7 us (0.84)
  Pallas kernels: 94.7 us -> 82.7 us
  local copies, waits for them, and re-layouts: 6.51 us -> 2.85 us
    pallas_call x1, Pallas kernels: 94.7 us -> 82.7 us  [step(): pl.pallas_call(functools.partial(kernel, geo), out_shape=(jax.ShapeDtypeS...]
    unnamed x12 -> x2, local copies, waits for them, and re-layouts: 6.51 us -> 2.85 us
where the time goes in v2:
time: 86.7 us; the launch traced here: 86.2 us
  Pallas kernels  82.7 us (95%)
  local copies, waits for them, and re-layouts  2.85 us (3%)
    pallas_call x1, Pallas kernels, step(): pl.pallas_call(functools.partial(kernel, geo), out_shape=(jax.ShapeDtypeS...  82.7 us
    unnamed x2, local copies, waits for them, and re-layouts  2.85 us

profile of v2, /device:TPU:6, one launch (start us, length us, event | category | flops | bytes accessed | tf_op | source)
XLA Modules:
  0.0 86.2 jit_solution(11046159422003094041)
XLA Ops:
  0.6 82.7 %shard_map.68 = (f32[4,4096]{1,0:T(4,128)}, f32[32,256]{1,0:T(8,128)}) custom-call(bf16[32,256]{1,0:T(8,128)(2,1)} %tf_hbm.1, bf16[32,256]{1,0:T(8,128)(2,1)} %sf_hbm.1, bf16[1,32]{1,0:T(2,128)(2,1)} %bitcast.1, bf16[256,4096]{1,0:T(8,128)(2,1)} %tv_hbm.1, bf16[256,4096]{1,0:T(8,128)(2,1)} %sv_hbm.1), custom_call_target="tpu_custom_call" | custom-call | tf_op jit(solution)/shard_map/pallas_call | solution.py:339
  83.4 1.5 %copy.9 = f32[4,4096]{1,0:T(4,128)} copy(f32[4,4096]{1,0:T(4,128)} %get-tuple-element.4) | data formatting | bytes 131072
  84.8 1.4 %copy.10 = f32[32,256]{1,0:T(8,128)} copy(f32[32,256]{1,0:T(8,128)} %get-tuple-element.5) | data formatting | bytes 65536

commit v3 on v2

--- a/solution.py
+++ b/solution.py
@@ -11,6 +11,9 @@
 ITERS = 3
 BLOCKS = 16
 HALF = BLOCKS // 2
+PARTS = 4
+WIDE = HALF // PARTS
+SKIP_FROM = 0
 
 teacher_temp = 0.04
 student_temp = 0.1
@@ -42,12 +45,12 @@
 
 def kernel(
     geo,
-    tf_hbm, sf_hbm, cw_ref, tv_hbm, sv_hbm,
+    tf_hbm, sf_hbm, cw_hbm, tv_hbm, sv_hbm,
     gv_ref, gf_ref,
-    tf, sf, tv, sv, sw, tu, su, sut, perm, mass, prob, winv, svec, rb, ab, bb, fg,
-    col_own, col_recv, row_own, row_recv, st_own, st_recv,
+    tf, sf, cw, tv, sv, sw, tu, su, sut, perm, mass, prob, winv, svec, rb, ab, bb, fg,
+    sums, col_own, col_recv, row_own, row_recv, st_own, st_recv,
     part, ring_recv, second, second_recv, fg_recv,
-    local_sem, gather_send, gather_recv, col_send, col_got, row_send, row_got, st_send, st_got,
+    local_sem, gather_send, gather_recv, col_sent, col_got, row_send, row_got, st_send, st_got,
     ring_send, ring_got, second_send, second_got, fg_send, fg_got,
 ):
     ny, nz, nf = geo
@@ -86,7 +89,7 @@
 
     loads = [
         pltpu.make_async_copy(src, dst, local_sem.at[i])
-        for i, (src, dst) in enumerate(((tf_hbm, tf), (sf_hbm, sf), (tv_hbm, tv), (sv_hbm, sv)))
+        for i, (src, dst) in enumerate(((tf_hbm, tf), (sf_hbm, sf), (tv_hbm, tv), (sv_hbm, sv), (cw_hbm, cw)))
     ]
     for load in loads:
         load.start()
@@ -153,57 +156,47 @@
         i = lax.broadcasted_iota(jnp.int32, (local, rows), 0)
         c = lax.broadcasted_iota(jnp.int32, (local, rows), 1)
         place = (c == f * local + i).astype(F32).astype(BF16)
-        st_own[1] = dot_nn(cw_ref[...], place)
+        loads[4].wait()
+        st_own[1] = dot_nn(cw[...], place)
         for j in far_first(nf):
             send(st_own, st_recv.at[j - 1], st_send, st_got, on_f(j))
 
-    def col_first(it, h):
-        axis, n, _ = axes[h]
+    def col_send(it, stage, sums):
+        col_own[it, stage] = sums.astype(BF16)
+        axis, n, _ = axes[stage]
         for j in far_first(n):
-            send(col_own.at[it, h, 0], col_recv.at[it, h, 0, j - 1], col_send.at[it, h, 0], col_got.at[it, h, 0], axis(j))
-
-    def col_total(it, h, stage):
-        n = axes[(h + stage) % 2][1]
-        took(col_recv.at[it, h, stage], col_got.at[it, h, stage])
-        total = col_own[it, h, stage]
-        for j in range(n - 1):
-            total = total + col_recv[it, h, stage, j]
+            send(col_own.at[it, stage], col_recv.at[it, stage, j - 1], col_sent.at[it, stage], col_got.at[it, stage], axis(j))
+
+    def col_total(it, stage):
+        took(col_recv.at[it, stage], col_got.at[it, stage])
+        total = col_own[it, stage].astype(F32)
+        for j in range(axes[stage][1] - 1):
+            total = total + col_recv[it, stage, j].astype(F32)
         return total
-
-    def col_second(it, h):
-        col_own[it, h, 1] = col_total(it, h, 0)
-        axis, n, _ = axes[1 - h]
-        for j in far_first(n):
-            send(col_own.at[it, h, 1], col_recv.at[it, h, 1, j - 1], col_send.at[it, h, 1], col_got.at[it, h, 1], axis(j))
 
     student_prototypes()
     took(tu.at[others], gather_recv.at[0])
     gather(1, su)
     for it in range(ITERS):
-        for h in range(2):
-            for k in range(HALF):
-                j = h * HALF + k
-                if it == 0:
-                    values = jnp.exp(dot_nn(tu[...], tv[:, block(j)]) * (1.0 / teacher_temp))
-                    mass[j] = values
-                else:
-                    values = mass[j] * rb[...]
-                col_own[it, h, 0, k : k + 1, :] = jnp.sum(values, axis=0, keepdims=True)
-
-            col_first(it, h)
+        for j in range(BLOCKS):
+            if it == 0:
+                values = jnp.exp(dot_nn(tu[...], tv[:, block(j)]) * (1.0 / teacher_temp))
+                mass[j] = values
+            else:
+                values = mass[j] * rb[...]
+            sums[j : j + 1, :] = jnp.sum(values, axis=0, keepdims=True)
+        col_send(it, 0, sums[...])
         if it == 0:
             student_orders()
-        for h in range(2):
-            col_second(it, h)
+        col_send(it, 1, col_total(it, 0))
         if it == 0:
             student_mass()
+        svec[...] = 1.0 / (col_total(it, 1) * protos)
         total = jnp.zeros((rows, 128), F32)
-        for h in range(2):
-            svec[h * HALF : (h + 1) * HALF, :] = 1.0 / (col_total(it, h, 1) * protos)
-            for j in range(h * HALF, (h + 1) * HALF):
-                values = mass[j] * svec[j : j + 1, :]
-                for c in range(0, cb, 128):
-                    total = total + values[:, c : c + 128]
+        for j in range(BLOCKS):
+            values = mass[j] * svec[j : j + 1, :]
+            for c in range(0, cb, 128):
+                total = total + values[:, c : c + 128]
         row_own[it] = lanes_of(total)
         for j in far_first(nf):
             send(row_own.at[it], row_recv.at[it, j - 1], row_send.at[it], row_got.at[it], on_f(j))
@@ -224,40 +217,57 @@
             bb[...] = rows_of(weights / (row_total * student_temp), cb)
 
     fg[...] = jnp.zeros_like(fg)
-    rings = [(h, q) for q in range(4) for h in range(2)]
+    rings = [(h, q) for q in range(PARTS) for h in range(2)]
 
     def chunk(h, c):
         size = bot // axes[h][1]
         return pl.ds(pl.multiple_of(c * size, size), size)
 
-    def lengths(h, q):
+    def length(h, q, way):
         n = axes[h][1]
-        return (n // 2, (n - 1) // 2) if q % 2 == 0 else ((n - 1) // 2, n // 2)
-
-    def chain_slot(h, q, way, s):
-        return s if way == 0 else lengths(h, q)[0] + s
-
-    def chain_step(h, q, way, s):
+        return n // 2 if way == q % 2 else (n - 1) // 2
+
+    def slot(h, q, way, far):
+        return (length(h, q, 0) if way else 0) + far - 1
+
+    def skips(h, q, way):
+        return length(h, q, way) % 2 == 0 and q >= SKIP_FROM
+
+    def senders(h, q, way, far):
+        n = length(h, q, way)
+        if skips(h, q, way) and far == n - 2:
+            return (n, n - 1)
+        if far == n or (skips(h, q, way) and far == n - 1):
+            return ()
+        return (far + 1,)
+
+    def chain_step(h, q, way, far):
         axis, n, me = axes[h]
-        r = 4 * h + q
-        left = lengths(h, q)[way] - s
-        c = lax.rem(me + (left if way == 0 else n - left), n)
-        if s > 0:
-            before = chain_slot(h, q, way, s - 1)
-            took(ring_recv.at[r, before], ring_got.at[r, before])
-            part[r, chunk(h, c), :] = part[r, chunk(h, c), :] + ring_recv[r, before]
-        now = chain_slot(h, q, way, s)
-        send(part.at[r, chunk(h, c)], ring_recv.at[r, now], ring_send.at[r], ring_got.at[r, now], axis(1 if way == 0 else n - 1))
+        r, last = PARTS * h + q, length(h, q, way)
+        rows_to = chunk(h, lax.rem(me + (far if way == 0 else n - far), n))
+        for sender in senders(h, q, way, far):
+            got = slot(h, q, way, sender)
+            took(ring_recv.at[r, got], ring_got.at[r, got])
+            part[r, rows_to, :] = part[r, rows_to, :] + ring_recv[r, got]
+        hops = 2 if skips(h, q, way) and far == last else 1
+        now = slot(h, q, way, far)
+        send(
+            part.at[r, rows_to], ring_recv.at[r, now], ring_send.at[r], ring_got.at[r, now],
+            axis(hops if way == 0 else n - hops),
+        )
 
     def chain_steps(h, q, s):
-        for way in (0, 1) if q % 2 == 0 else (1, 0):
-            if s < lengths(h, q)[way]:
-                chain_step(h, q, way, s)
+        for way in (q % 2, 1 - q % 2):
+            last = length(h, q, way)
+            for far in range(last, 0, -1):
+                at = max(last - far - 1, 0) if skips(h, q, way) else last - far
+                if at == s:
+                    chain_step(h, q, way, far)
 
     for h, q in rings:
-        r = 4 * h + q
-        for k in range(2):
-            j = 2 * r + k
+        r = PARTS * h + q
+        for k in range(WIDE):
+            j = WIDE * r + k
             g = (prob[j] * ab[...] - mass[j] * bb[...] * svec[j : j + 1, :]).astype(BF16)
             fg[...] += dot_nt(g, sw[:, block(j)])
             grad = dot_nn(sut[h], g)
@@ -279,19 +289,21 @@
     each = bot // (ny * nz)
     for h in range(2):
         _, n, me = axes[h]
-        sums = []
-        for q in range(4):
-            r = 4 * h + q
+        totals = []
+        for q in range(PARTS):
+            r = PARTS * h + q
             total = part[r, chunk(h, me), :].astype(F32)
             for way in range(2):
-                if lengths(h, q)[way]:
-                    last = chain_slot(h, q, way, lengths(h, q)[way] - 1)
-                    took(ring_recv.at[r, last], ring_got.at[r, last])
-                    total = total + ring_recv[r, last].astype(F32)
-            sums.append(total)
+                for sender in senders(h, q, way, 0):
+                    got = slot(h, q, way, sender)
+                    took(ring_recv.at[r, got], ring_got.at[r, got])
+                    total = total + ring_recv[r, got].astype(F32)
+            totals.append(total)
+        totals = jnp.concatenate(totals, axis=1)
+        totals = [totals[:, k * cb : (k + 2) * cb] for k in range(0, HALF, 2)]
         axis, n2, me2 = axes[1 - h]
         for c in range(n2):
-            second[h, c] = jnp.concatenate([total[c * each : (c + 1) * each] for total in sums], axis=0).astype(BF16)
+            second[h, c] = jnp.concatenate([total[c * each : (c + 1) * each] for total in totals], axis=0).astype(BF16)
         for j in far_first(n2):
             send(second.at[h, lax.rem(me2 + j, n2)], second_recv.at[h, j - 1], second_send.at[h], second_got.at[h], axis(j))
 
@@ -315,16 +327,20 @@
     for i, unit in enumerate((tu, su)):
         took(unit.at[others], gather_send.at[i])
     for it in range(ITERS):
-        for h in range(2):
-            for stage in range(2):
-                took(col_recv.at[it, h, stage], col_send.at[it, h, stage])
+        for stage in range(2):
+            took(col_recv.at[it, stage], col_sent.at[it, stage])
         took(row_recv.at[it], row_send.at[it])
     took(st_recv, st_send)
     took(fg_recv, fg_send)
     for h in range(2):
-        for r in range(4 * h, 4 * h + 4):
+        for r in range(PARTS * h, PARTS * (h + 1)):
             took(ring_recv.at[r], ring_send.at[r])
         took(second_recv.at[h], second_send.at[h])
+
+
+def hand_over(gv_ref, gf_ref, gv_out, gf_out):
+    gv_out[...] = gv_ref[...]
+    gf_out[...] = gf_ref[...]
 
 
 def step(geo, teacher_feat, student_feat, crop_weight, teacher_v, student_v):
@@ -336,17 +352,18 @@
     any_space = pl.BlockSpec(memory_space=pl.ANY)
     vmem = pl.BlockSpec(memory_space=pltpu.VMEM)
     dma = pltpu.SemaphoreType.DMA
-    return pl.pallas_call(
+    grads = pl.pallas_call(
         functools.partial(kernel, geo),
         out_shape=(
             jax.ShapeDtypeStruct((each, kl), F32),
             jax.ShapeDtypeStruct((local, bot), F32),
         ),
-        in_specs=[any_space, any_space, vmem, any_space, any_space],
+        in_specs=[any_space] * 5,
         out_specs=(vmem, vmem),
         scratch_shapes=[
             pltpu.VMEM((local, bot), BF16),
             pltpu.VMEM((local, bot), BF16),
+            pltpu.VMEM((1, local), BF16),
             pltpu.VMEM((bot, kl), BF16),
             pltpu.VMEM((bot, kl), BF16),
             pltpu.VMEM((bot, kl), BF16),
@@ -362,23 +379,24 @@
             pltpu.VMEM((rows, cb), F32),
             pltpu.VMEM((rows, cb), F32),
             pltpu.VMEM((rows, bot), F32),
-            pltpu.VMEM((ITERS, 2, 2, HALF, cb), F32),
-            pltpu.VMEM((ITERS, 2, 2, ny - 1, HALF, cb), F32),
+            pltpu.VMEM((BLOCKS, cb), F32),
+            pltpu.VMEM((ITERS, 2, BLOCKS, cb), BF16),
+            pltpu.VMEM((ITERS, 2, ny - 1, BLOCKS, cb), BF16),
             pltpu.VMEM((ITERS, 1, rows), F32),
             pltpu.VMEM((ITERS, nf - 1, 1, rows), F32),
             pltpu.VMEM((2, 1, rows), F32),
             pltpu.VMEM((nf - 1, 2, 1, rows), F32),
-            pltpu.VMEM((8, bot, 2 * cb), BF16),
-            pltpu.VMEM((8, ny - 1, bot // ny, 2 * cb), BF16),
+            pltpu.VMEM((2 * PARTS, bot, WIDE * cb), BF16),
+            pltpu.VMEM((2 * PARTS, ny - 1, bot // ny, WIDE * cb), BF16),
             pltpu.VMEM((2, ny, 4 * each, 2 * cb), BF16),
             pltpu.VMEM((2, ny - 1, 4 * each, 2 * cb), BF16),
             pltpu.VMEM((nf - 1, local, bot), F32),
-            dma((4,)),
+            dma((5,)),
             dma((2,)), dma((2,)),
-            dma((ITERS, 2, 2)), dma((ITERS, 2, 2)),
+            dma((ITERS, 2)), dma((ITERS, 2)),
             dma((ITERS,)), dma((ITERS,)),
             dma, dma,
-            dma((8,)), dma((8, ny - 1)),
+            dma((2 * PARTS,)), dma((2 * PARTS, ny - 1)),
             dma((2,)), dma((2,)),
             dma, dma,
         ],
@@ -386,6 +404,12 @@
             collective_id=0, has_side_effects=True, vmem_limit_bytes=62 * 1024 * 1024
         ),
     )(teacher_feat, student_feat, crop_weight.reshape(1, local), teacher_v, student_v)
+    return pl.pallas_call(
+        hand_over,
+        out_shape=[jax.ShapeDtypeStruct(grad.shape, grad.dtype) for grad in grads],
+        in_specs=[vmem, vmem],
+        out_specs=[vmem, vmem],
+    )(*grads)
 
 
 def solution(mesh, planes=(8, 8)):

time: 86.7 us -> 84.5 us (0.975)
  local copies, waits for them, and re-layouts: 2.85 us -> 0 us
  Pallas kernels: 82.7 us -> 83.7 us
    unnamed x2 -> x0, local copies, waits for them, and re-layouts: 2.85 us -> none
    pallas_call x0 -> x1, Pallas kernels: none -> 1.48 us  [step(): pl.pallas_call(hand_over, out_shape=[jax.ShapeDtypeStruct(grad.shape, gra...]
where the time goes in v3:
time: 84.5 us; the launch traced here: 84.3 us
  Pallas kernels  83.7 us (99%)
    pallas_call x1, Pallas kernels, step(): pl.pallas_call(functools.partial(kernel, geo), out_shape=(jax.ShapeDtypeS...  82.2 us

profile of v3, /device:TPU:6, one launch (start us, length us, event | category | flops | bytes accessed | tf_op | source)
XLA Modules:
  0.0 84.3 jit_solution(5846631424230397626)
XLA Ops:
  0.6 82.2 %shard_map.68 = (f32[4,4096]{1,0:T(4,128)}, f32[32,256]{1,0:T(8,128)}) custom-call(bf16[32,256]{1,0:T(8,128)(2,1)} %tf_hbm.1, bf16[32,256]{1,0:T(8,128)(2,1)} %sf_hbm.1, bf16[1,32]{1,0:T(2,128)(2,1)} %bitcast.1, bf16[256,4096]{1,0:T(8,128)(2,1)} %tv_hbm.1, bf16[256,4096]{1,0:T(8,128)(2,1)} %sv_hbm.1), custom_call_target="tpu_custom_call" | custom-call | tf_op jit(solution)/shard_map/pallas_call | solution.py:355
  82.9 1.5 %shard_map.69 = (f32[4,4096]{1,0:T(4,128)}, f32[32,256]{1,0:T(8,128)}) custom-call(f32[4,4096]{1,0:T(4,128)} %get-tuple-element.4.gv_ref, f32[32,256]{1,0:T(8,128)} %get-tuple-element.5.gf_ref), custom_call_target="tpu_custom_call" | custom-call | tf_op jit(solution)/shard_map/pallas_call | solution.py:407

commit v4 on v3

--- a/solution.py
+++ b/solution.py
@@ -13,7 +13,14 @@
 HALF = BLOCKS // 2
 PARTS = 4
 WIDE = HALF // PARTS
-SKIP_FROM = 0
+ROUTES = (1, 1, 1, 2)
+TOWARDS = {
+    0: ((), (), ()),
+    1: ((0,), (0,), (0,)),
+    2: ((0, 1), (0, 0), (0, 0)),
+    3: ((0, 1, 2), (0, 1, 2), (0, 0, 2)),
+    4: ((0, 1, 2, 3), (0, 1, 2, 2), (0, 0, 2, 2)),
+}
 
 teacher_temp = 0.04
 student_temp = 0.1
@@ -50,7 +57,7 @@
     tf, sf, cw, tv, sv, sw, tu, su, sut, perm, mass, prob, winv, svec, rb, ab, bb, fg,
     sums, col_own, col_recv, row_own, row_recv, st_own, st_recv,
     part, ring_recv, second, second_recv, fg_recv,
-    local_sem, gather_send, gather_recv, col_sent, col_got, row_send, row_got, st_send, st_got,
+    told, local_sem, gather_send, gather_recv, col_sent, col_got, row_send, row_got, st_send, st_got,
     ring_send, ring_got, second_send, second_got, fg_send, fg_got,
 ):
     ny, nz, nf = geo
@@ -94,9 +101,11 @@
     for load in loads:
         load.start()
     barrier = pltpu.get_barrier_semaphore()
-    for axis, n in ((on_f, nf), (on_y, ny), (on_z, nz)):
-        for j in far_first(n):
-            pl.semaphore_signal(barrier, inc=1, device_id=axis(j), device_id_type=MESH)
+    greeted = [on_f(j) for j in far_first(nf)]
+    for axis, n, _ in axes:
+        greeted += [axis(j) for j in sorted({1, n - 1})]
+    for device in greeted:
+        pl.semaphore_signal(barrier, inc=1, device_id=device, device_id_type=MESH)
 
     own = pl.ds(pl.multiple_of(f * local, local), local)
 
@@ -109,13 +118,24 @@
     tu[own, :] = unit_rows(tf)[0].astype(BF16)
     loads[1].wait()
     su[own, :] = unit_rows(sf)[0].astype(BF16)
-    pl.semaphore_wait(barrier, nf + ny + nz - 3)
+    pl.semaphore_wait(barrier, len(greeted))
+
+    def tell(reach):
+        for a, (axis, n, _) in enumerate(axes):
+            for j in (reach, n - reach) if 2 * reach < n else ():
+                pl.semaphore_signal(told.at[a, reach // 2], inc=1, device_id=axis(j), device_id_type=MESH)
+
+    def hear(reach):
+        for a, (_, n, _) in enumerate(axes):
+            if 2 * reach < n:
+                pl.semaphore_wait(told.at[a, reach // 2], 2)
 
     def gather(i, unit):
         for j in far_first(nf):
             send(unit.at[own], unit.at[own], gather_send.at[i], gather_recv.at[i], on_f(j))
 
     gather(0, tu)
+    tell(1)
     others = pl.ds(0, rows - local)
 
     loads[2].wait()
@@ -123,6 +143,8 @@
         values = tv[:, block(j)].astype(F32)
         inverse = 1.0 / jnp.sqrt(jnp.sum(values * values, axis=0, keepdims=True) + epsilon)
         tv[:, block(j)] = (values * inverse).astype(BF16)
+    hear(1)
+    tell(2)
 
     def student_prototypes():
         loads[3].wait()
@@ -175,6 +197,7 @@
         return total
 
     student_prototypes()
+    hear(2)
     took(tu.at[others], gather_recv.at[0])
     gather(1, su)
     for it in range(ITERS):
@@ -230,26 +253,24 @@
     def slot(h, q, way, far):
         return (length(h, q, 0) if way else 0) + far - 1
 
-    def skips(h, q, way):
-        return length(h, q, way) % 2 == 0 and q >= SKIP_FROM
+    def towards(h, q, way, far):
+        return TOWARDS[length(h, q, way)][ROUTES[q]][far - 1]
 
     def senders(h, q, way, far):
-        n = length(h, q, way)
-        if skips(h, q, way) and far == n - 2:
-            return (n, n - 1)
-        if far == n or (skips(h, q, way) and far == n - 1):
-            return ()
-        return (far + 1,)
+        return [other for other in range(length(h, q, way), far, -1) if towards(h, q, way, other) == far]
+
+    def depth(h, q, way, far):
+        return 0 if far == 0 else 1 + depth(h, q, way, towards(h, q, way, far))
 
     def chain_step(h, q, way, far):
         axis, n, me = axes[h]
-        r, last = PARTS * h + q, length(h, q, way)
+        r = PARTS * h + q
         rows_to = chunk(h, lax.rem(me + (far if way == 0 else n - far), n))
         for sender in senders(h, q, way, far):
             got = slot(h, q, way, sender)
             took(ring_recv.at[r, got], ring_got.at[r, got])
             part[r, rows_to, :] = part[r, rows_to, :] + ring_recv[r, got]
-        hops = 2 if skips(h, q, way) and far == last else 1
+        hops = far - towards(h, q, way, far)
         now = slot(h, q, way, far)
         send(
             part.at[r, rows_to], ring_recv.at[r, now], ring_send.at[r], ring_got.at[r, now],
@@ -258,10 +279,10 @@
 
     def chain_steps(h, q, s):
         for way in (q % 2, 1 - q % 2):
-            last = length(h, q, way)
-            for far in range(last, 0, -1):
-                at = max(last - far - 1, 0) if skips(h, q, way) else last - far
-                if at == s:
+            far_ones = range(length(h, q, way), 0, -1)
+            steps = max([depth(h, q, way, far) for far in far_ones], default=0)
+            for far in far_ones:
+                if steps - depth(h, q, way, far) == s:
                     chain_step(h, q, way, far)
 
     for h, q in rings:
@@ -391,6 +412,7 @@
             pltpu.VMEM((2, ny, 4 * each, 2 * cb), BF16),
             pltpu.VMEM((2, ny - 1, 4 * each, 2 * cb), BF16),
             pltpu.VMEM((nf - 1, local, bot), F32),
+            pltpu.SemaphoreType.REGULAR((2, 2)),
             dma((5,)),
             dma((2,)), dma((2,)),
             dma((ITERS, 2)), dma((ITERS, 2)),

time: 84.5 us -> 82.4 us (0.975)
  Pallas kernels: 83.7 us -> 81.3 us
    pallas_call x1, Pallas kernels: 82.2 us -> 79.8 us  [step(): pl.pallas_call(functools.partial(kernel, geo), out_shape=(jax.ShapeDtypeS...]
where the time goes in v4:
time: 82.4 us; the launch traced here: 81.9 us
  Pallas kernels  81.3 us (99%)
    pallas_call x1, Pallas kernels, step(): pl.pallas_call(functools.partial(kernel, geo), out_shape=(jax.ShapeDtypeS...  79.8 us

profile of v4, /device:TPU:6, one launch (start us, length us, event | category | flops | bytes accessed | tf_op | source)
XLA Modules:
  0.0 81.9 jit_solution(11378098349109974210)
XLA Ops:
  0.6 79.8 %shard_map.68 = (f32[4,4096]{1,0:T(4,128)}, f32[32,256]{1,0:T(8,128)}) custom-call(bf16[32,256]{1,0:T(8,128)(2,1)} %tf_hbm.1, bf16[32,256]{1,0:T(8,128)(2,1)} %sf_hbm.1, bf16[1,32]{1,0:T(2,128)(2,1)} %bitcast.1, bf16[256,4096]{1,0:T(8,128)(2,1)} %tv_hbm.1, bf16[256,4096]{1,0:T(8,128)(2,1)} %sv_hbm.1), custom_call_target="tpu_custom_call" | custom-call | tf_op jit(solution)/shard_map/pallas_call | solution.py:376
  80.4 1.5 %shard_map.69 = (f32[4,4096]{1,0:T(4,128)}, f32[32,256]{1,0:T(8,128)}) custom-call(f32[4,4096]{1,0:T(4,128)} %get-tuple-element.4.gv_ref, f32[32,256]{1,0:T(8,128)} %get-tuple-element.5.gf_ref), custom_call_target="tpu_custom_call" | custom-call | tf_op jit(solution)/shard_map/pallas_call | solution.py:429

commit v5 on v4

--- a/solution.py
+++ b/solution.py
@@ -98,14 +98,14 @@
         pltpu.make_async_copy(src, dst, local_sem.at[i])
         for i, (src, dst) in enumerate(((tf_hbm, tf), (sf_hbm, sf), (tv_hbm, tv), (sv_hbm, sv), (cw_hbm, cw)))
     ]
-    for load in loads:
-        load.start()
     barrier = pltpu.get_barrier_semaphore()
     greeted = [on_f(j) for j in far_first(nf)]
     for axis, n, _ in axes:
         greeted += [axis(j) for j in sorted({1, n - 1})]
     for device in greeted:
         pl.semaphore_signal(barrier, inc=1, device_id=device, device_id_type=MESH)
+    for i in (0, 2, 1, 4, 3):
+        loads[i].start()
 
     own = pl.ds(pl.multiple_of(f * local, local), local)
 
@@ -116,8 +116,6 @@
 
     loads[0].wait()
     tu[own, :] = unit_rows(tf)[0].astype(BF16)
-    loads[1].wait()
-    su[own, :] = unit_rows(sf)[0].astype(BF16)
     pl.semaphore_wait(barrier, len(greeted))
 
     def tell(reach):
@@ -136,6 +134,8 @@
 
     gather(0, tu)
     tell(1)
+    loads[1].wait()
+    su[own, :] = unit_rows(sf)[0].astype(BF16)
     others = pl.ds(0, rows - local)
 
     loads[2].wait()
@@ -160,14 +160,16 @@
         d = lax.broadcasted_iota(jnp.int32, (bot, bot), 1)
         pz, py, pi = p // (ny * each), lax.rem(p // each, ny), lax.rem(p, each)
         perm[...] = (d == (py * nz + pz) * each + pi).astype(F32).astype(BF16)
+        for j in range(HALF, BLOCKS):
+            sv[:, block(j)] = dot_nn(perm[...], sv[:, block(j)]).astype(BF16)
+
+    def student_mass():
         took(su.at[others], gather_recv.at[1])
         units = su[...]
+        p = lax.broadcasted_iota(jnp.int32, (bot, bot), 0)
+        d = lax.broadcasted_iota(jnp.int32, (bot, bot), 1)
         sut[0] = dot_nt((d == p).astype(F32).astype(BF16), units).astype(BF16)
         sut[1] = dot_nt(perm[...], units).astype(BF16)
-        for j in range(HALF, BLOCKS):
-            sv[:, block(j)] = dot_nn(perm[...], sv[:, block(j)]).astype(BF16)
-
-    def student_mass():
         total = jnp.zeros((rows, 128), F32)
         for j in range(BLOCKS):
             values = jnp.exp(dot_nn(su[...], sw[:, block(j)]) * (1.0 / student_temp))
@@ -196,10 +198,8 @@
             total = total + col_recv[it, stage, j].astype(F32)
         return total
 
-    student_prototypes()
     hear(2)
     took(tu.at[others], gather_recv.at[0])
-    gather(1, su)
     for it in range(ITERS):
         for j in range(BLOCKS):
             if it == 0:
@@ -210,6 +210,8 @@
             sums[j : j + 1, :] = jnp.sum(values, axis=0, keepdims=True)
         col_send(it, 0, sums[...])
         if it == 0:
+            gather(1, su)
+            student_prototypes()
             student_orders()
         col_send(it, 1, col_total(it, 0))
         if it == 0:
@@ -218,6 +220,8 @@
         total = jnp.zeros((rows, 128), F32)
         for j in range(BLOCKS):
             values = mass[j] * svec[j : j + 1, :]
+            if it == ITERS - 1:
+                mass[j] = values
             for c in range(0, cb, 128):
                 total = total + values[:, c : c + 128]
         row_own[it] = lanes_of(total)
@@ -230,6 +234,8 @@
                 student_total = student_total + st_recv[j, 0]
                 weights = weights + st_recv[j, 1]
             ab[...] = rows_of(weights / (student_total * student_temp), cb)
+            for j in range(BLOCKS):
+                prob[j] = prob[j] * ab[...]
         took(row_recv.at[it], row_got.at[it])
         row_total = row_own[it]
         for j in range(nf - 1):
@@ -289,7 +295,7 @@
         r = PARTS * h + q
         for k in range(WIDE):
             j = WIDE * r + k
-            g = (prob[j] * ab[...] - mass[j] * bb[...] * svec[j : j + 1, :]).astype(BF16)
+            g = (prob[j] - mass[j] * bb[...]).astype(BF16)
             fg[...] += dot_nt(g, sw[:, block(j)])
             grad = dot_nn(sut[h], g)
             inverse = winv[j : j + 1, :]
@@ -335,16 +341,6 @@
     hat, length = unit_rows(sf)
     gf_ref[...] = (grad - hat * jnp.sum(hat * grad, axis=1, keepdims=True)) / length
 
-    for h in range(2):
-        took(second_recv.at[h], second_got.at[h])
-        _, n2, me2 = axes[1 - h]
-        total = second[h, me2].astype(F32)
-        for j in range(n2 - 1):
-            total = total + second_recv[h, j].astype(F32)
-        for q in range(4):
-            first = h * HALF * cb + q * 2 * cb
-            gv_ref[:, first : first + 2 * cb] = total[q * each : (q + 1) * each]
-
     for i, unit in enumerate((tu, su)):
         took(unit.at[others], gather_send.at[i])
     for it in range(ITERS):
@@ -356,6 +352,17 @@
     for h in range(2):
         for r in range(PARTS * h, PARTS * (h + 1)):
             took(ring_recv.at[r], ring_send.at[r])
+
+    for h in range(2):
+        took(second_recv.at[h], second_got.at[h])
+        _, n2, me2 = axes[1 - h]
+        total = second[h, me2].astype(F32)
+        for j in range(n2 - 1):
+            total = total + second_recv[h, j].astype(F32)
+        for q in range(4):
+            first = h * HALF * cb + q * 2 * cb
+            gv_ref[:, first : first + 2 * cb] = total[q * each : (q + 1) * each]
+    for h in range(2):
         took(second_recv.at[h], second_send.at[h])
 
 

time: 82.4 us -> 82.2 us (level)
  no operation moved by 1% of the time
where the time goes in v5:
time: 82.2 us; the launch traced here: 81.9 us
  Pallas kernels  81.2 us (99%)
    pallas_call x1, Pallas kernels, step(): pl.pallas_call(functools.partial(kernel, geo), out_shape=(jax.ShapeDtypeS...  79.8 us

profile of v5, /device:TPU:6, one launch (start us, length us, event | category | flops | bytes accessed | tf_op | source)
XLA Modules:
  0.0 81.9 jit_solution(14589640093560056179)
XLA Ops:
  0.6 79.8 %shard_map.68 = (f32[4,4096]{1,0:T(4,128)}, f32[32,256]{1,0:T(8,128)}) custom-call(bf16[32,256]{1,0:T(8,128)(2,1)} %tf_hbm.1, bf16[32,256]{1,0:T(8,128)(2,1)} %sf_hbm.1, bf16[1,32]{1,0:T(2,128)(2,1)} %bitcast.1, bf16[256,4096]{1,0:T(8,128)(2,1)} %tv_hbm.1, bf16[256,4096]{1,0:T(8,128)(2,1)} %sv_hbm.1), custom_call_target="tpu_custom_call" | custom-call | tf_op jit(solution)/shard_map/pallas_call | solution.py:383
  80.4 1.5 %shard_map.69 = (f32[4,4096]{1,0:T(4,128)}, f32[32,256]{1,0:T(8,128)}) custom-call(f32[4,4096]{1,0:T(4,128)} %get-tuple-element.4.gv_ref, f32[32,256]{1,0:T(8,128)} %get-tuple-element.5.gf_ref), custom_call_target="tpu_custom_call" | custom-call | tf_op jit(solution)/shard_map/pallas_call | solution.py:436
